TPU v7x, 32 devices: a whole 2x2x4 slice. The times are simulated.
32 devices in a mesh: grp: 4 (over y, core), dev: 8 (over z, x).
Axes of the slice: x: 2, y: 2, z: 4, core: 2. Of those that a mesh axis runs over, the one named last changes fastest.
Arguments:
- points: bfloat16 [12288, 128], P(('grp', 'dev')), may hold values from -6 to 6
- start_vectors: float32 [12288, 32], P(('grp', 'dev')), may hold values from -6 to 6
Outputs:
- embedding: float32 [12288, 32], P(('grp', 'dev'))
All inputs are finite; a program needn't handle non-finite values.
Results may differ from a plain program's by a relative error of at most 0.005.
Values may be sent and summed in bfloat16 or wider, within the bound.
A program may use at most 128 MiB of HBM per device.

v0:
```python
import math
import jax
import jax.numpy as jnp
from jax import lax
from jax.sharding import PartitionSpec as P

ITERS = 2
sharpness = 8.0
panels_per_block = 16


def unit_rows(points):
    values = points.astype(jnp.float32)
    squares = jnp.sum(values * values, axis=-1, keepdims=True)
    return (values * lax.rsqrt(squares + 1e-06)).astype(jnp.bfloat16)


def tile_weights(own_units, others):
    cosine = lax.dot_general(
        own_units, others, (((1,), (1,)), ((), ())), preferred_element_type=jnp.float32
    )
    return jnp.exp(sharpness * (cosine - 1.0)).astype(jnp.bfloat16)


def weight_panel(own_units, rolled, count):
    tile_rows = own_units.shape[0]
    width = panels_per_block * tile_rows

    def fill(index, panel):
        others = lax.dynamic_slice_in_dim(rolled, index * width, width, 0)
        return lax.dynamic_update_slice_in_dim(
            panel, tile_weights(own_units, others), index * width, 1
        )

    empty = jnp.zeros((tile_rows, count * tile_rows), jnp.bfloat16)
    return lax.fori_loop(0, count // panels_per_block, fill, empty)


def share_iterate(iterate):
    return lax.all_gather(iterate, ("grp", "dev"), axis=0, tiled=True)


def orthonormal(image):
    gram_local = jnp.dot(
        image.T, image, precision=lax.Precision.HIGHEST, preferred_element_type=jnp.float32
    )
    gram_total = lax.psum(gram_local, ("grp", "dev"))
    factor = jnp.linalg.cholesky(gram_total)
    return lax.linalg.triangular_solve(factor, image.T, left_side=True, lower=True).T


def body(points, start_vectors):
    tile_rows = points.shape[0]
    panels = lax.axis_size(("grp", "dev"))
    position = lax.axis_index(("grp", "dev"))
    own_units = unit_rows(points)
    all_units = lax.all_gather(own_units, ("grp", "dev"), axis=0, tiled=True)
    rolled = jnp.roll(all_units, -position * tile_rows, axis=0)
    vectors = start_vectors
    weights = weight_panel(own_units, rolled, panels)
    degree = jnp.sum(weights, axis=1, dtype=jnp.float32)
    scale = lax.rsqrt(degree)[:, None]
    for sweep in range(ITERS):
        iterate = (scale * vectors).astype(jnp.bfloat16)
        gathered = jnp.roll(share_iterate(iterate), -position * tile_rows, axis=0)
        product = jnp.dot(weights, gathered, preferred_element_type=jnp.float32)
        vectors = orthonormal(scale * product)
    return vectors * math.sqrt(tile_rows * panels)


def solution(mesh):
    placed = (P(("grp", "dev"), None), P(("grp", "dev"), None))
    return jax.shard_map(
        body, mesh=mesh, in_specs=placed, out_specs=P(("grp", "dev"), None), check_vma=False
    )
```

profile of v0, /device:TPU:14, one launch (start us, length us, event | category | flops | bytes accessed | tf_op | source)
XLA Modules:
  0.0 340.0 jit_solution(12517805892950426013)
XLA Ops:
  6.5 1.0 fusion.12
  7.6 1.7 fusion.13
  9.3 59.4 %all-gather.2.cloned.1.call-done = bf16[12288,128]{1,0:T(8,128)(2,1)} async-done(((bf16[384,128]{1,0:T(8,128)(2,1)}), bf16[12288,128]{1,0:T(8,128)(2,1)}) %all-gather.2.cloned.1.call-update) | async-done | bytes 3145744 | tf_op jit(solution)/shard_map/all_gather | solution.py:57
  68.6 4.2 %fusion.4 = bf16[12288,128]{1,0:T(8,128)(2,1)S(1)} fusion(s32[]{:T(128)S(6)} %select_n.35, bf16[12288,128]{1,0:T(8,128)(2,1)} %all-gather.2.cloned.1.call-done), kind=kLoop, calls=%fused_computation.8 | loop fusion | flops 6291456 | bytes 6291460 | tf_op jit(solution)/shard_map/jit(_roll_dynamic)/concatenate | solution.py:58
  72.9 4.4 %broadcast_in_dim.2 = bf16[384,12288]{0,1:T(8,128)(2,1)} broadcast(bf16[]{:T(256)} %constant.130.clone.1), dimensions={} | broadcast | bytes 9437186 | tf_op jit(solution)/shard_map/broadcast_in_dim | solution.py:35
  77.3 7.7 %while.15 = (s32[]{:T(128)}, bf16[384,12288]{0,1:T(8,128)(2,1)}, bf16[12288,128]{1,0:T(8,128)(2,1)S(1)}, bf16[384,128]{1,0:T(8,128)(2,1)S(1)}, s32[]{:T(128)}, /*index=5*/s32[]{:T(128)}, s32[]{:T(128)}, s32[]{:T(128)}) while((s32[]{:T(128)}, bf16[384,12288]{0,1:T(8,128)(2,1)}, bf16[12288,128]{1,0:T(8,128)(2,1)S(1)}, ...), condition=%wide.region_2.3_spmd, body=%wide.region_1.2_spmd.sunk | while | flops 611057664 | bytes 6390915 | solution.py:36
  77.3 3.8 %fusion.42 = bf16[384,12288]{0,1:T(8,128)(2,1)} fusion(bf16[384,12288]{0,1:T(8,128)(2,1)} %get-tuple-element.161, s32[]{:T(128)S(6)} %select_n.52, bf16[384,128]{1,0:T(8,128)(2,1)S(1)} %get-tuple-element.171, bf16[12288,128]{1,0:T(8,128)(2,1)S(1)} %get-tuple-element.170), kind=kOutput, calls=%fused_computation.2.clone.1 | convolution fusion | flops 611057664 | bytes 6390784 | tf_op jit(solution)/shard_map/while/body/eval_jaxpr/dot_general | solution.py:19
  81.1 3.9 %fusion.42 = bf16[384,12288]{0,1:T(8,128)(2,1)} fusion(bf16[384,12288]{0,1:T(8,128)(2,1)} %get-tuple-element.161, s32[]{:T(128)S(6)} %select_n.52, bf16[384,128]{1,0:T(8,128)(2,1)S(1)} %get-tuple-element.171, bf16[12288,128]{1,0:T(8,128)(2,1)S(1)} %get-tuple-element.170), kind=kOutput, calls=%fused_computation.2.clone.1 | convolution fusion | flops 611057664 | bytes 6390784 | tf_op jit(solution)/shard_map/while/body/eval_jaxpr/dot_general | solution.py:19
  85.0 6.4 %convert_reduce_fusion = f32[384]{0:T(512)S(1)} fusion(bf16[384,12288]{0,1:T(8,128)(2,1)} %get-tuple-element.118), kind=kLoop, calls=%fused_computation.5 | loop fusion | flops 9436800 | bytes 9438720 | tf_op jit(solution)/shard_map/reduce_sum | solution.py:61
  91.5 68.2 %all_gather.10 = bf16[12288,32]{0,1:T(8,128)(2,1)S(1)} all-gather(bf16[384,32]{0,1:T(8,128)(2,1)S(1)} %multiply_convert_fusion), channel_id=1, replica_groups=mesh['grp'=4,'dev'=8] {'grp','dev'}, dimensions={0}, use_global_device_ids=true | all-gather | bytes 811008 | tf_op jit(solution)/shard_map/all_gather | solution.py:40
  159.7 1.7 convolution_multiply_fusion.1
  161.6 43.7 %psum.14 = f32[32,32]{0,1:T(8,128)S(1)} all-reduce(f32[32,32]{0,1:T(8,128)S(1)} %fusion.28), channel_id=1, replica_groups=mesh['grp'=4,'dev'=8] {'grp','dev'}, use_global_device_ids=true, to_apply=%region_4.6 | all-reduce | flops 1024 | bytes 8192 | tf_op jit(solution)/shard_map/psum | solution.py:47
  205.4 2.9 cholesky.44
  208.3 0.6 compare_reduce_fusion.1
  209.0 0.7 fusion.16
  209.6 2.4 custom-call.6
  212.3 64.6 %all_gather.11 = bf16[12288,32]{0,1:T(8,128)(2,1)S(1)} all-gather(bf16[384,32]{0,1:T(8,128)(2,1)S(1)} %fusion.7), channel_id=1, replica_groups=mesh['grp'=4,'dev'=8] {'grp','dev'}, dimensions={0}, use_global_device_ids=true | all-gather | bytes 811008 | tf_op jit(solution)/shard_map/all_gather | solution.py:40
  276.9 5.4 %convolution_multiply_fusion = f32[384,32]{0,1:T(8,128)S(1)} fusion(bf16[384,12288]{0,1:T(8,128)(2,1)} %get-tuple-element.118, s32[]{:T(128)S(6)} %select_n.35, bf16[12288,32]{0,1:T(8,128)(2,1)S(1)} %all_gather.11, f32[384]{0:T(512)S(1)} %rsqrt.16), kind=kOutput, calls=%fused_computation.13 | convolution fusion | flops 303575040 | bytes 10274308 | tf_op jit(solution)/shard_map/dot_general | solution.py:66
  282.5 43.0 %psum.15 = f32[32,32]{0,1:T(8,128)S(1)} all-reduce(f32[32,32]{0,1:T(8,128)S(1)} %fusion.29), channel_id=1, replica_groups=mesh['grp'=4,'dev'=8] {'grp','dev'}, use_global_device_ids=true, to_apply=%region_7.11 | all-reduce | flops 1024 | bytes 8192 | tf_op jit(solution)/shard_map/psum | solution.py:47
  325.6 2.9 cholesky.55
  328.5 0.6 compare_reduce_fusion
  329.2 0.7 fusion.17
  329.8 2.4 custom-call.7
  332.3 0.9 fusion.5
  (20 shorter events, 0.9 us)
Async XLA Ops:
  6.5 62.1 %all-gather.2.cloned.1.call-start = ((), (), s32[]{:S(2)}) async-start(), calls=%async_computation | async-start | bytes 3244032 | tf_op jit(solution)/shard_map/all_gather | solution.py:57
  72.9 4.4 %copy-start.1 = (bf16[384,128]{1,0:T(8,128)(2,1)S(1)}, bf16[384,128]{1,0:T(8,128)(2,1)}, u32[]{:S(2)}) copy-start(bf16[384,128]{1,0:T(8,128)(2,1)} %fusion.13) | copy-start | bytes 294916
  77.3 14.1 %copy-start.2 = (f32[384,32]{0,1:T(8,128)S(1)}, f32[384,32]{0,1:T(8,128)}, u32[]{:S(2)}) copy-start(f32[384,32]{0,1:T(8,128)} %param.10) | copy-start | bytes 147460
  85.0 74.7 %copy-start = (bf16[384,12288]{0,1:T(8,128)(2,1)S(1)}, bf16[384,12288]{0,1:T(8,128)(2,1)}, u32[]{:S(2)}) copy-start(bf16[384,12288]{0,1:T(8,128)(2,1)} %get-tuple-element.118) | copy-start | bytes 28311556
Sparse Core Ops, SparseCore 0:
  10.3 58.2 all-gather.1
where the time goes:
time: 341 us; the launch traced here: 340 us
  blocking collectives  219 us (64%)
  waiting for transfers between devices  59.4 us (17%)
  other arithmetic  26.7 us (8%)
  matrix products  16.3 us (5%)
  between operations  13.5 us (4%)
  local copies, waits for them, and re-layouts  4.56 us (1%)
    all_gather x2, blocking collectives, share_iterate(): return lax.all_gather(iterate, ('grp', 'dev'), axis=0, tiled=True)  133 us
    psum x2, blocking collectives, orthonormal(): gram_total = lax.psum(gram_local, ('grp', 'dev'))  86.7 us
    all_gather x1, waiting for transfers between devices, body(): all_units = lax.all_gather(own_units, ('grp', 'dev'), axis=0, tiled=True)  59.4 us
    dot_general x2, matrix products, tile_weights(): lax.dot_general(own_units, others, (((1,), (1,)), ((), ())), preferred_el...  7.69 us
    another operation x6, other arithmetic, orthonormal(): factor = jnp.linalg.cholesky(gram_total)  7.19 us
    dot_general x2, matrix products, body(): product = jnp.dot(weights, gathered, preferred_element_type=jnp.float32)  7.09 us
  transfers between devices with their start and end apart: 1, of which 1 were waited for; matrix products, arithmetic and copies ran while one was open for 0% of the time, Pallas kernels for 0%

commit v1 on v0

--- a/solution.py
+++ b/solution.py
@@ -44,7 +44,7 @@
     gram_local = jnp.dot(
         image.T, image, precision=lax.Precision.HIGHEST, preferred_element_type=jnp.float32
     )
-    gram_total = lax.psum(gram_local, ("grp", "dev"))
+    gram_total = jnp.sum(lax.all_gather(gram_local, ("grp", "dev")), 0)
     factor = jnp.linalg.cholesky(gram_total)
     return lax.linalg.triangular_solve(factor, image.T, left_side=True, lower=True).T
 

time: 341 us -> 398 us (1.17)
  blocking collectives: 219 us -> 274 us
    all_gather x0 -> x2, blocking collectives: none -> 138 us  [orthonormal(): gram_total = jnp.sum(lax.all_gather(gram_local, ('grp', 'dev')), 0)]
    psum x2 -> x0, blocking collectives: 86.7 us -> none  [orthonormal(): gram_total = lax.psum(gram_local, ('grp', 'dev'))]
where the time goes in v1:
time: 398 us; the launch traced here: 395 us
  blocking collectives  274 us (69%)
  waiting for transfers between devices  59.4 us (15%)
  other arithmetic  26.8 us (7%)
  matrix products  16.3 us (4%)
  between operations  13.5 us (3%)
  local copies, waits for them, and re-layouts  4.56 us (1%)
    all_gather x2, blocking collectives, orthonormal(): gram_total = jnp.sum(lax.all_gather(gram_local, ('grp', 'dev')), 0)  138 us
    all_gather x2, blocking collectives, share_iterate(): return lax.all_gather(iterate, ('grp', 'dev'), axis=0, tiled=True)  136 us
    all_gather x1, waiting for transfers between devices, body(): all_units = lax.all_gather(own_units, ('grp', 'dev'), axis=0, tiled=True)  59.4 us
  transfers between devices with their start and end apart: 1, of which 1 were waited for; matrix products, arithmetic and copies ran while one was open for 0% of the time, Pallas kernels for 0%

profile of v1, /device:TPU:14, one launch (start us, length us, event | category | flops | bytes accessed | tf_op | source)
XLA Modules:
  0.0 394.8 jit_solution(2802606807349853417)
XLA Ops:
  6.5 1.0 fusion.12
  7.6 1.7 fusion.13
  9.3 59.4 %all-gather.4.cloned.1.call-done = bf16[12288,128]{1,0:T(8,128)(2,1)} async-done(((bf16[384,128]{1,0:T(8,128)(2,1)}), bf16[12288,128]{1,0:T(8,128)(2,1)}) %all-gather.4.cloned.1.call-update) | async-done | bytes 3145744 | tf_op jit(solution)/shard_map/all_gather | solution.py:57
  68.6 4.2 %fusion.4 = bf16[12288,128]{1,0:T(8,128)(2,1)S(1)} fusion(s32[]{:T(128)S(6)} %select_n.35, bf16[12288,128]{1,0:T(8,128)(2,1)} %all-gather.4.cloned.1.call-done), kind=kLoop, calls=%fused_computation.8 | loop fusion | flops 6291456 | bytes 6291460 | tf_op jit(solution)/shard_map/jit(_roll_dynamic)/concatenate | solution.py:58
  72.9 4.4 %broadcast_in_dim.2 = bf16[384,12288]{0,1:T(8,128)(2,1)} broadcast(bf16[]{:T(256)} %constant.130.clone.1), dimensions={} | broadcast | bytes 9437186 | tf_op jit(solution)/shard_map/broadcast_in_dim | solution.py:35
  77.3 7.7 %while.15 = (s32[]{:T(128)}, bf16[384,12288]{0,1:T(8,128)(2,1)}, bf16[12288,128]{1,0:T(8,128)(2,1)S(1)}, bf16[384,128]{1,0:T(8,128)(2,1)S(1)}, s32[]{:T(128)}, /*index=5*/s32[]{:T(128)}, s32[]{:T(128)}, s32[]{:T(128)}) while((s32[]{:T(128)}, bf16[384,12288]{0,1:T(8,128)(2,1)}, bf16[12288,128]{1,0:T(8,128)(2,1)S(1)}, ...), condition=%wide.region_2.3_spmd, body=%wide.region_1.2_spmd.sunk | while | flops 611057664 | bytes 6390915 | solution.py:36
  77.3 3.8 fusion.42
  81.1 3.9 fusion.42
  85.0 6.4 %convert_reduce_fusion = f32[384]{0:T(512)S(1)} fusion(bf16[384,12288]{0,1:T(8,128)(2,1)} %get-tuple-element.118), kind=kLoop, calls=%fused_computation.5 | loop fusion | flops 9436800 | bytes 9438720 | tf_op jit(solution)/shard_map/reduce_sum | solution.py:61
  91.5 68.2 %all_gather.22 = bf16[12288,32]{0,1:T(8,128)(2,1)S(1)} all-gather(bf16[384,32]{0,1:T(8,128)(2,1)S(1)} %multiply_convert_fusion), channel_id=1, replica_groups=mesh['grp'=4,'dev'=8] {'grp','dev'}, dimensions={0}, use_global_device_ids=true | all-gather | bytes 811008 | tf_op jit(solution)/shard_map/all_gather | solution.py:40
  159.7 1.7 convolution_multiply_fusion.1
  161.6 69.1 %all-gather = f32[1024,32]{1,0:T(8,128)S(1)} all-gather(f32[32,32]{1,0:T(8,128)S(1)} %fusion.28), channel_id=2, replica_groups=mesh['grp'=4,'dev'=8] {'grp','dev'}, dimensions={0}, use_global_device_ids=true | all-gather | bytes 135168 | tf_op jit(solution)/shard_map/all_gather | solution.py:47
  230.8 2.9 cholesky.44
  233.8 0.6 compare_reduce_fusion.1
  234.4 0.7 fusion.16
  235.1 2.4 custom-call.6
  237.8 67.9 %all_gather.25 = bf16[12288,32]{0,1:T(8,128)(2,1)S(1)} all-gather(bf16[384,32]{0,1:T(8,128)(2,1)S(1)} %fusion.7), channel_id=1, replica_groups=mesh['grp'=4,'dev'=8] {'grp','dev'}, dimensions={0}, use_global_device_ids=true | all-gather | bytes 811008 | tf_op jit(solution)/shard_map/all_gather | solution.py:40
  305.7 5.4 %convolution_multiply_fusion = f32[384,32]{0,1:T(8,128)S(1)} fusion(bf16[384,12288]{0,1:T(8,128)(2,1)} %get-tuple-element.118, s32[]{:T(128)S(6)} %select_n.35, bf16[12288,32]{0,1:T(8,128)(2,1)S(1)} %all_gather.25, f32[384]{0:T(512)S(1)} %rsqrt.16), kind=kOutput, calls=%fused_computation.13 | convolution fusion | flops 303575040 | bytes 10274308 | tf_op jit(solution)/shard_map/dot_general | solution.py:66
  311.2 69.0 %all-gather.1 = f32[1024,32]{1,0:T(8,128)S(1)} all-gather(f32[32,32]{1,0:T(8,128)S(1)} %fusion.29), channel_id=3, replica_groups=mesh['grp'=4,'dev'=8] {'grp','dev'}, dimensions={0}, use_global_device_ids=true | all-gather | bytes 135168 | tf_op jit(solution)/shard_map/all_gather | solution.py:47
  380.4 2.9 cholesky.55
  383.4 0.6 compare_reduce_fusion
  384.0 0.7 fusion.17
  384.7 2.4 custom-call.7
  387.1 0.9 fusion.5
  (22 shorter events, 1.0 us)
Async XLA Ops:
  6.5 62.1 %all-gather.4.cloned.1.call-start = ((), (), s32[]{:S(2)}) async-start(), calls=%async_computation | async-start | bytes 3244032 | tf_op jit(solution)/shard_map/all_gather | solution.py:57
  72.9 4.4 %copy-start.1 = (bf16[384,128]{1,0:T(8,128)(2,1)S(1)}, bf16[384,128]{1,0:T(8,128)(2,1)}, u32[]{:S(2)}) copy-start(bf16[384,128]{1,0:T(8,128)(2,1)} %fusion.13) | copy-start | bytes 294916
  77.3 14.1 %copy-start.2 = (f32[384,32]{0,1:T(8,128)S(1)}, f32[384,32]{0,1:T(8,128)}, u32[]{:S(2)}) copy-start(f32[384,32]{0,1:T(8,128)} %param.10) | copy-start | bytes 147460
  85.0 74.7 %copy-start = (bf16[384,12288]{0,1:T(8,128)(2,1)S(1)}, bf16[384,12288]{0,1:T(8,128)(2,1)}, u32[]{:S(2)}) copy-start(bf16[384,12288]{0,1:T(8,128)(2,1)} %get-tuple-element.118) | copy-start | bytes 28311556
Sparse Core Ops, SparseCore 0:
  10.3 58.2 all-gather.3

commit v2 on v0

--- a/solution.py
+++ b/solution.py
@@ -44,7 +44,9 @@
     gram_local = jnp.dot(
         image.T, image, precision=lax.Precision.HIGHEST, preferred_element_type=jnp.float32
     )
-    gram_total = lax.psum(gram_local, ("grp", "dev"))
+    gram_total = gram_local
+    for dev in ("dev", "grp"):
+        gram_total = lax.psum(gram_total, dev)
     factor = jnp.linalg.cholesky(gram_total)
     return lax.linalg.triangular_solve(factor, image.T, left_side=True, lower=True).T
 

time: 341 us -> 351 us (1.029)
  the two profiles are of different devices: /device:TPU:14 before, /device:TPU:0 now
where the time goes in v2:
time: 351 us
  blocking collectives  227 us (65%)
  waiting for transfers between devices  62.9 us (18%)
  other arithmetic  26.8 us (8%)
  matrix products  16.3 us (5%)
  between operations  13.5 us (4%)
  local copies, waits for them, and re-layouts  4.56 us (1%)
    all_gather x2, blocking collectives, share_iterate(): return lax.all_gather(iterate, ('grp', 'dev'), axis=0, tiled=True)  139 us
    psum x4, blocking collectives, orthonormal(): gram_total = lax.psum(gram_total, dev)  87.8 us
    all_gather x1, waiting for transfers between devices, body(): all_units = lax.all_gather(own_units, ('grp', 'dev'), axis=0, tiled=True)  62.8 us
    dot_general x2, matrix products, tile_weights(): lax.dot_general(own_units, others, (((1,), (1,)), ((), ())), preferred_el...  7.7 us
    another operation x6, other arithmetic, orthonormal(): factor = jnp.linalg.cholesky(gram_total)  7.19 us
    dot_general x2, matrix products, body(): product = jnp.dot(weights, gathered, preferred_element_type=jnp.float32)  7.1 us
  transfers between devices with their start and end apart: 1, of which 1 were waited for; matrix products, arithmetic and copies ran while one was open for 0% of the time, Pallas kernels for 0%

profile of v2, /device:TPU:0, one launch (start us, length us, event | category | flops | bytes accessed | tf_op | source)
XLA Modules:
  0.0 350.9 jit_solution(7912149055157934587)
XLA Ops:
  6.5 1.0 fusion.12
  7.6 1.7 fusion.13
  9.3 62.8 %all-gather.2.cloned.1.call-done = bf16[12288,128]{1,0:T(8,128)(2,1)} async-done(((bf16[384,128]{1,0:T(8,128)(2,1)}), bf16[12288,128]{1,0:T(8,128)(2,1)}) %all-gather.2.cloned.1.call-update) | async-done | bytes 3145744 | tf_op jit(solution)/shard_map/all_gather | solution.py:59
  72.1 4.3 %fusion.4 = bf16[12288,128]{1,0:T(8,128)(2,1)S(1)} fusion(s32[]{:T(128)S(6)} %select_n.35, bf16[12288,128]{1,0:T(8,128)(2,1)} %all-gather.2.cloned.1.call-done), kind=kLoop, calls=%fused_computation.8 | loop fusion | flops 6291456 | bytes 6291460 | tf_op jit(solution)/shard_map/jit(_roll_dynamic)/concatenate | solution.py:60
  76.4 4.4 %broadcast_in_dim.2 = bf16[384,12288]{0,1:T(8,128)(2,1)} broadcast(bf16[]{:T(256)} %constant.130.clone.1), dimensions={} | broadcast | bytes 9437186 | tf_op jit(solution)/shard_map/broadcast_in_dim | solution.py:35
  80.8 7.7 %while.15 = (s32[]{:T(128)}, bf16[384,12288]{0,1:T(8,128)(2,1)}, bf16[12288,128]{1,0:T(8,128)(2,1)S(1)}, bf16[384,128]{1,0:T(8,128)(2,1)S(1)}, s32[]{:T(128)}, /*index=5*/s32[]{:T(128)}, s32[]{:T(128)}, s32[]{:T(128)}) while((s32[]{:T(128)}, bf16[384,12288]{0,1:T(8,128)(2,1)}, bf16[12288,128]{1,0:T(8,128)(2,1)S(1)}, ...), condition=%wide.region_2.3_spmd, body=%wide.region_1.2_spmd.sunk | while | flops 611057664 | bytes 6390915 | solution.py:36
  80.8 3.8 %fusion.42 = bf16[384,12288]{0,1:T(8,128)(2,1)} fusion(bf16[384,12288]{0,1:T(8,128)(2,1)} %get-tuple-element.161, s32[]{:T(128)S(6)} %select_n.52, bf16[384,128]{1,0:T(8,128)(2,1)S(1)} %get-tuple-element.171, bf16[12288,128]{1,0:T(8,128)(2,1)S(1)} %get-tuple-element.170), kind=kOutput, calls=%fused_computation.2.clone.1 | convolution fusion | flops 611057664 | bytes 6390784 | tf_op jit(solution)/shard_map/while/body/eval_jaxpr/dot_general | solution.py:19
  84.7 3.9 %fusion.42 = bf16[384,12288]{0,1:T(8,128)(2,1)} fusion(bf16[384,12288]{0,1:T(8,128)(2,1)} %get-tuple-element.161, s32[]{:T(128)S(6)} %select_n.52, bf16[384,128]{1,0:T(8,128)(2,1)S(1)} %get-tuple-element.171, bf16[12288,128]{1,0:T(8,128)(2,1)S(1)} %get-tuple-element.170), kind=kOutput, calls=%fused_computation.2.clone.1 | convolution fusion | flops 611057664 | bytes 6390784 | tf_op jit(solution)/shard_map/while/body/eval_jaxpr/dot_general | solution.py:19
  88.5 6.4 %convert_reduce_fusion = f32[384]{0:T(512)S(1)} fusion(bf16[384,12288]{0,1:T(8,128)(2,1)} %get-tuple-element.118), kind=kLoop, calls=%fused_computation.5 | loop fusion | flops 9436800 | bytes 9438720 | tf_op jit(solution)/shard_map/reduce_sum | solution.py:63
  95.0 70.7 %all_gather.10 = bf16[12288,32]{0,1:T(8,128)(2,1)S(1)} all-gather(bf16[384,32]{0,1:T(8,128)(2,1)S(1)} %multiply_convert_fusion), channel_id=1, replica_groups=mesh['grp'=4,'dev'=8] {'grp','dev'}, dimensions={0}, use_global_device_ids=true | all-gather | bytes 811008 | tf_op jit(solution)/shard_map/all_gather | solution.py:40
  165.7 1.7 convolution_multiply_fusion.1
  167.6 33.0 %psum.28 = f32[32,32]{0,1:T(8,128)S(1)} all-reduce(f32[32,32]{0,1:T(8,128)S(1)} %fusion.28), channel_id=1, replica_groups=mesh['grp'=4,'dev'=8] {'dev'}, use_global_device_ids=true, to_apply=%region_4.6 | all-reduce | flops 1024 | bytes 8192 | tf_op jit(solution)/shard_map/psum | solution.py:49
  200.6 10.1 %psum.29 = f32[32,32]{0,1:T(8,128)S(1)} all-reduce(f32[32,32]{0,1:T(8,128)S(1)} %psum.28), channel_id=1, replica_groups=mesh['grp'=4,'dev'=8] {'grp'}, use_global_device_ids=true, to_apply=%region_5.7 | all-reduce | flops 1024 | bytes 8192 | tf_op jit(solution)/shard_map/psum | solution.py:49
  210.8 2.9 cholesky.44
  214.4 0.7 fusion.16
  215.1 2.4 custom-call.6
  217.8 68.4 %all_gather.11 = bf16[12288,32]{0,1:T(8,128)(2,1)S(1)} all-gather(bf16[384,32]{0,1:T(8,128)(2,1)S(1)} %fusion.7), channel_id=1, replica_groups=mesh['grp'=4,'dev'=8] {'grp','dev'}, dimensions={0}, use_global_device_ids=true | all-gather | bytes 811008 | tf_op jit(solution)/shard_map/all_gather | solution.py:40
  286.1 5.4 %convolution_multiply_fusion = f32[384,32]{0,1:T(8,128)S(1)} fusion(bf16[384,12288]{0,1:T(8,128)(2,1)} %get-tuple-element.118, s32[]{:T(128)S(6)} %select_n.35, bf16[12288,32]{0,1:T(8,128)(2,1)S(1)} %all_gather.11, f32[384]{0:T(512)S(1)} %rsqrt.16), kind=kOutput, calls=%fused_computation.13 | convolution fusion | flops 303575040 | bytes 10274308 | tf_op jit(solution)/shard_map/dot_general | solution.py:68
  291.7 34.6 %psum.30 = f32[32,32]{0,1:T(8,128)S(1)} all-reduce(f32[32,32]{0,1:T(8,128)S(1)} %fusion.29), channel_id=1, replica_groups=mesh['grp'=4,'dev'=8] {'dev'}, use_global_device_ids=true, to_apply=%region_8.12 | all-reduce | flops 1024 | bytes 8192 | tf_op jit(solution)/shard_map/psum | solution.py:49
  326.3 10.1 %psum.31 = f32[32,32]{0,1:T(8,128)S(1)} all-reduce(f32[32,32]{0,1:T(8,128)S(1)} %psum.30), channel_id=1, replica_groups=mesh['grp'=4,'dev'=8] {'grp'}, use_global_device_ids=true, to_apply=%region_9.13 | all-reduce | flops 1024 | bytes 8192 | tf_op jit(solution)/shard_map/psum | solution.py:49
  336.5 2.9 cholesky.55
  340.1 0.7 fusion.17
  340.7 2.4 custom-call.7
  343.2 0.9 fusion.5
  (22 shorter events, 2.2 us)
Async XLA Ops:
  6.5 65.6 %all-gather.2.cloned.1.call-start = ((), (), s32[]{:S(2)}) async-start(), calls=%async_computation | async-start | bytes 3244032 | tf_op jit(solution)/shard_map/all_gather | solution.py:59
  76.4 4.4 %copy-start.1 = (bf16[384,128]{1,0:T(8,128)(2,1)S(1)}, bf16[384,128]{1,0:T(8,128)(2,1)}, u32[]{:S(2)}) copy-start(bf16[384,128]{1,0:T(8,128)(2,1)} %fusion.13) | copy-start | bytes 294916
  80.8 14.1 %copy-start.2 = (f32[384,32]{0,1:T(8,128)S(1)}, f32[384,32]{0,1:T(8,128)}, u32[]{:S(2)}) copy-start(f32[384,32]{0,1:T(8,128)} %param.10) | copy-start | bytes 147460
  88.5 77.1 %copy-start = (bf16[384,12288]{0,1:T(8,128)(2,1)S(1)}, bf16[384,12288]{0,1:T(8,128)(2,1)}, u32[]{:S(2)}) copy-start(bf16[384,12288]{0,1:T(8,128)(2,1)} %get-tuple-element.118) | copy-start | bytes 28311556
Sparse Core Ops, SparseCore 0:
  10.3 61.7 all-gather.1
